TPU v7x, 256 devices: a whole 4x4x8 slice. The times are simulated.
256 devices in a mesh: feed: 4 (over z_lo, core), chan: 64 (over x, y, z_hi).
Axes of the slice: x: 4, y: 4, z: 8 (z_hi: 4, z_lo: 2; z = z_hi * 2 + z_lo), core: 2. Of those that a mesh axis runs over, the one named last changes fastest.
Arguments:
- voltages: bfloat16 [4, 2, 8192, 40, 512], P('feed', None, 'chan'), may hold values from -6 to 6
- fine_delays: int32 [32, 8192], replicated, may hold values from 0 to 8, as said below
- coarse_delays: int32 [1024, 64], replicated, may hold values from 0 to 16, as said below
Outputs:
- candidates: float32 [4, 512, 1024], P(None, ('feed', 'chan'))
Inputs may be any that keep to these rules, and one draw needn't show every extreme that they name: `fine_delays`: every row reaches 8. `coarse_delays`: every row reaches 16.
All inputs are finite; a program needn't handle non-finite values.
Results may differ from a plain program's by a relative error of at most 0.0003.
Values sent between devices are 32-bit elements; how exact they have to be, the bound alone decides.
A program may use at most 128 MiB of HBM per device.

v0:
```python
import jax
import jax.numpy as jnp
from jax import lax
from jax.sharding import PartitionSpec as P

FINE_MAX = 8
COARSE_MAX = 16
NWID = 4


epsilon = 1e-06


def boxcar_search(series, total_channels):
    results = []
    box = series
    width = 1
    for level in range(NWID):
        results.append(jnp.max(box, axis=1) / jnp.sqrt(jnp.float32(width * total_channels)))
        if level + 1 < NWID:
            box = box[:, :-width] + box[:, width:]
            width = width * 2
    return jnp.stack(results)


def local(voltages, fine_delays, coarse_delays):
    summed = lax.psum_scatter(
        voltages[0].astype(jnp.float32), "feed", scatter_dimension=3, tiled=True
    )
    power = summed[0] * summed[0] + summed[1] * summed[1]
    level = jnp.mean(power, axis=1, keepdims=True)
    intensity = jnp.transpose(power / (level + epsilon) - 1.0, (1, 2, 0))
    groups = fine_delays.shape[0]
    samples = intensity.shape[0]
    band_width = intensity.shape[2]
    span = samples - FINE_MAX
    whole = lax.all_to_all(intensity, "chan", split_axis=1, concat_axis=2, tiled=True)
    bands = lax.axis_size("chan")
    beam_count = whole.shape[1]
    cube = whole.reshape(samples, beam_count, bands, band_width)
    marks = fine_delays.reshape(groups, bands, band_width)
    partial_value = jnp.zeros((bands, beam_count, span, groups), jnp.float32)
    for delay in range(FINE_MAX + 1):
        chosen = (marks == delay).astype(jnp.float32)
        partial_value = partial_value + jnp.einsum(
            "tbsc,gsc->sbtg", cube[delay : delay + span], chosen, precision=lax.Precision.HIGHEST
        )
    bands = partial_value.shape[0]
    beam_count = partial_value.shape[1]
    length = span - COARSE_MAX
    trials = coarse_delays.shape[0]
    per_group = trials // groups
    codes = coarse_delays.reshape(groups, per_group, bands)
    series = jnp.zeros((beam_count, length, groups, per_group), jnp.float32)
    for delay in range(COARSE_MAX + 1):
        chosen = (codes == delay).astype(jnp.float32)
        series = series + jnp.einsum(
            "sbtg,gjs->btgj",
            partial_value[:, :, delay : delay + length],
            chosen,
            precision=lax.Precision.HIGHEST,
        )
    series = series.reshape(beam_count, length, trials)
    return boxcar_search(series, fine_delays.shape[1])


def solution(mesh):
    in_specs = (P("feed", None, "chan", None, None), P(), P())
    out_specs = P(None, ("feed", "chan"), None)
    return jax.shard_map(local, mesh=mesh, in_specs=in_specs, out_specs=out_specs, check_vma=False)
```

profile of v0, /device:TPU:32, one launch (start us, length us, event | category | flops | bytes accessed | tf_op | source)
XLA Modules:
  0.0 400.6 jit_solution(3758007361592252984)
XLA Ops:
  6.5 17.8 %copy.233 = bf16[1,2,128,40,512]{2,3,1,4,0:T(8,128)(2,1)} copy(bf16[1,2,128,40,512]{4,3,2,1,0:T(8,128)(2,1)} %param.3) | data formatting | bytes 20971520 | tf_op args[0]
  24.4 12.6 %bitcast_convert_fusion = f32[2,128,40,512]{1,2,0,3:T(8,128)} fusion(bf16[1,2,128,40,512]{2,3,1,4,0:T(8,128)(2,1)} %copy.233), kind=kLoop, calls=%fused_computation | loop fusion | flops 5242880 | bytes 31457280 | tf_op jit(solution)/shard_map/convert_element_type | solution.py:28
  37.0 183.9 %reduce-scatter.2.cloned.1.call-done = f32[2,128,40,128]{1,2,0,3:T(8,128)} async-done(((f32[2,128,40,512]{1,2,0,3:T(8,128)}), f32[2,128,40,128]{1,2,0,3:T(8,128)}) %reduce-scatter.2.cloned.1.call-update) | async-done | bytes 5242896 | tf_op jit(solution)/shard_map/reduce_scatter | solution.py:27
  221.0 3.5 fusion.33
  225.0 2.0 fusion.2
  227.0 13.9 %all-to-all-start = ((f32[40,128,128]{2,0,1:T(8,128)}), f32[40,128,128]{2,0,1:T(8,128)S(1)}, u32[]{:S(2)}, u32[]{:S(2)}) async-start(f32[40,128,128]{2,0,1:T(8,128)} %fusion.2), calls=%async_computation.1 | async-start | bytes 5242880 | tf_op jit(solution)/shard_map/all_to_all | solution.py:37
  241.0 2.6 compare_bitcast_fusion.8
  243.7 0.8 copy.325
  244.5 0.8 copy.324
  245.3 0.8 copy.323
  246.2 0.8 copy.330
  247.0 0.8 copy.329
  247.8 0.8 copy.328
  248.6 0.8 copy.327
  249.5 0.8 copy.322
  250.3 1.1 copy.232
  251.4 2.3 broadcast_compare_fusion
  253.8 53.4 %all-to-all-done = f32[40,128,128]{2,0,1:T(8,128)S(1)} async-done(((f32[40,128,128]{2,0,1:T(8,128)}), f32[40,128,128]{2,0,1:T(8,128)S(1)}, u32[]{:S(2)}, u32[]{:S(2)}) %all-to-all-start) | async-done | bytes 2621472 | tf_op jit(solution)/shard_map/all_to_all | solution.py:37
  307.2 1.3 fusion.11
  308.5 1.3 fusion.13
  309.9 1.3 fusion.15
  311.2 1.4 fusion.17
  312.6 1.3 fusion.3
  313.9 13.8 %fusion.5 = f32[64,32,32,2]{1,2,3,0:T(8,128)S(1)} fusion(f32[40,2,64,128]{3,0,1,2:T(8,128)S(1)} %bitcast.195, pred[32,64,128,1]{2,1,0,3:T(32,128)(4,1)S(1)} %bitcast.223), kind=kOutput, calls=%fused_computation.9 | convolution fusion | flops 201326592 | bytes 2883584 | tf_op jit(solution)/shard_map/tbsc,gsc->sbtg/dot_general | solution.py:45
  327.7 1.4 fusion.7
  329.1 1.4 fusion.9
  330.5 2.4 add_bitcast_fusion
  333.0 5.2 %fusion.37 = (f32[64,2,16,32]{3,2,1,0:T(8,128)S(1)}, f32[64,2,16,32]{3,2,1,0:T(8,128)S(1)}, f32[64,2,16,32]{3,2,1,0:T(8,128)S(1)}, f32[64,2,16,32]{3,2,1,0:T(8,1...) fusion(f32[64,2,32,32]{3,2,1,0:T(8,128)S(1)} %add_bitcast_fusion), kind=kLoop, calls=%fused_computation.91 | loop fusion | bytes 8912896 | tf_op jit(solution)/shard_map/slice | solution.py:59
  338.2 2.7 copy.243
  340.9 2.7 copy.245
  343.6 2.7 copy.247
  346.4 2.7 copy.249
  349.1 2.7 copy.251
  351.8 2.7 copy.253
  354.5 2.7 copy.255
  357.3 2.7 copy.257
  360.0 2.7 copy.259
  362.7 2.7 copy.261
  365.4 2.7 copy.263
  368.1 2.7 copy.265
  370.8 2.7 copy.267
  373.5 2.7 copy.269
  376.3 1.6 copy.271
  377.8 0.8 copy.273
  378.6 0.8 copy.275
  379.4 1.8 fusion.39
  381.3 1.5 convolution_add_fusion.15
  392.9 0.6 pad_maximum_fusion
  (104 shorter events, 10.3 us)
Async XLA Ops:
  6.5 214.4 %reduce-scatter.2.cloned.1.call-start = ((), (), s32[]{:S(2)}) async-start(), calls=%async_computation.2 | async-start | bytes 26214400 | tf_op jit(solution)/shard_map/reduce_scatter | solution.py:27
  221.0 4.1 %copy-start = (f32[2,128,40,128]{1,2,0,3:T(8,128)S(1)}, f32[2,128,40,128]{1,2,0,3:T(8,128)}, u32[]{:S(2)}) copy-start(f32[2,128,40,128]{1,2,0,3:T(8,128)} %reduce-scatter.2.cloned.1.call-done) | copy-start | bytes 15728644
  227.0 80.1 %all-to-all-start = ((f32[40,128,128]{2,0,1:T(8,128)}), f32[40,128,128]{2,0,1:T(8,128)S(1)}, u32[]{:S(2)}, u32[]{:S(2)}) async-start(f32[40,128,128]{2,0,1:T(8,128)} %fusion.2), calls=%async_computation.1 | async-start | bytes 5242880 | tf_op jit(solution)/shard_map/all_to_all | solution.py:37
  307.2 1.3 copy-start.15
  308.5 1.3 copy-start.16
  309.9 1.4 copy-start.17
  311.2 1.4 copy-start.18
  312.6 1.3 copy-start.36
  313.9 13.8 %copy-start.37 = (pred[4,8,64,128]{3,2,1,0:T(32,128)(4,1)S(1)}, pred[4,8,64,128]{3,2,1,0:T(32,128)(4,1)}, u32[]{:S(2)}) copy-start(pred[4,8,64,128]{3,2,1,0:T(32,128)(4,1)} %copy.328) | copy-start | bytes 786436
  327.7 1.4 copy-start.19
  329.1 1.4 copy-start.20
  377.8 3.5 copy-start.14
  378.6 4.2 %copy-start.13 = (f32[64,2,16,32]{0,2,1,3:T(8,128)S(1)}, f32[64,2,16,32]{0,2,1,3:T(8,128)}, u32[]{:S(2)}) copy-start(f32[64,2,16,32]{0,2,1,3:T(8,128)} %copy.247) | copy-start | bytes 786436
  378.6 4.2 %copy-start.35 = (pred[1024,64]{1,0:T(32,128)(4,1)S(1)}, pred[1024,64]{1,0:T(32,128)(4,1)}, u32[]{:S(2)}) copy-start(pred[1024,64]{1,0:T(32,128)(4,1)} %get-tuple-element.49) | copy-start | bytes 196612
  379.4 4.0 copy-start.12
  379.4 4.0 copy-start.34
  382.8 1.3 copy-start.11
  382.8 1.3 copy-start.33
  383.4 1.3 copy-start.10
  383.4 1.3 copy-start.32
  384.0 1.3 copy-start.9
  384.0 1.3 copy-start.31
  384.6 1.3 copy-start.8
  384.6 1.3 copy-start.30
  385.2 1.3 copy-start.7
  385.2 1.3 copy-start.29
  385.9 1.3 copy-start.6
  385.9 1.3 copy-start.28
  386.5 1.3 copy-start.5
  386.5 1.3 copy-start.27
  387.1 1.3 copy-start.4
  387.1 1.3 copy-start.26
  387.7 1.3 copy-start.3
  387.7 1.3 copy-start.25
  388.3 1.3 copy-start.2
  388.3 1.3 copy-start.24
  388.9 1.2 copy-start.1
  389.0 1.2 copy-start.23
  389.6 1.2 copy-start.22
  390.2 1.2 copy-start.21
Sparse Core Ops, SparseCore 0:
  37.1 183.7 reduce-scatter.1
where the time goes:
time: 406 us; the launch traced here: 401 us
  waiting for transfers between devices  237 us (58%)
  local copies, waits for them, and re-layouts  73.4 us (18%)
  matrix products  37.5 us (9%)
  other arithmetic  23.8 us (6%)
  between operations  14.5 us (4%)
  starting transfers between devices  13.9 us (3%)
    reduce_scatter x1, waiting for transfers between devices, local(): lax.psum_scatter(voltages[0].astype(jnp.float32), 'feed', scatter_dimensi...  184 us
    all_to_all x1, waiting for transfers between devices, local(): lax.all_to_all(intensity, 'chan', split_axis=1, concat_axis=2, tiled=True)  53.4 us
    slice x18, local copies, waits for them, and re-layouts, local(): partial_value[:, :, delay:delay + length]  46.4 us
    unnamed x87, local copies, waits for them, and re-layouts  26.4 us
    dot_general x9, matrix products, local(): jnp.einsum('tbsc,gsc->sbtg', cube[delay:delay + span], chosen, precision=...  25.6 us
    all_to_all x1, starting transfers between devices, local(): lax.all_to_all(intensity, 'chan', split_axis=1, concat_axis=2, tiled=True)  13.9 us
    convert_element_type x1, other arithmetic, local(): voltages[0].astype(jnp.float32)  12.6 us
    dot_general x17, matrix products, local(): jnp.einsum('sbtg,gjs->btgj', partial_value[:, :, delay:delay + length], c...  12 us
  transfers between devices with their start and end apart: 2, of which 2 were waited for; matrix products, arithmetic and copies ran while one was open for 3% of the time, Pallas kernels for 0%

commit v1 on v0

v1 whole, which is shorter than its diff:
```python
import functools
import math

import jax
import jax.numpy as jnp
from jax import lax
from jax.experimental import pallas as pl
from jax.experimental.pallas import tpu as pltpu
from jax.sharding import PartitionSpec as P

FINE_MAX = 8
COARSE_MAX = 16
NWID = 4
MESH = pl.DeviceIdType.MESH

epsilon = 1e-06
PART = 8
BLOCK = 16
LANES = 128


def gather_lanes(x, index):
    numbers = lax.GatherDimensionNumbers(
        offset_dims=(),
        collapsed_slice_dims=(1,),
        start_index_map=(1,),
        operand_batching_dims=(0,),
        start_indices_batching_dims=(0,),
    )
    return lax.gather(
        x, index[..., None], numbers, (1, 1), mode=lax.GatherScatterMode.PROMISE_IN_BOUNDS
    )


def kernel(
    bands, total_channels,
    v_hbm, fine_hbm, coarse_hbm, out_ref,
    v, s1, r1, r2, xt, xhl, mask, fd, cd, cdt, idx, o, m, r3,
    load_sem, side_sem, d_send, d_recv, z_send, z_recv, a_send, a_recv,
):
    parts = v.shape[1]
    samples = v.shape[4]
    lanes = v.shape[5]
    rows = PART * samples
    groups = fd.shape[0]
    width = fd.shape[1]
    span = samples - FINE_MAX
    per_group = cd.shape[0] // groups
    rowsets = cd.shape[0] // LANES
    feed = lax.axis_index("feed")
    me = lax.axis_index("chan")
    core, low = lax.rem(feed, 2), lax.div(feed, 2)

    def quarter(r):
        return lax.rem(low + r // 2, 2) * 2 + lax.rem(core + r % 2, 2)

    core_peer, chip_peer = quarter(1), quarter(2)

    def load(i, r):
        return pltpu.make_async_copy(
            v_hbm.at[0, :, pl.ds(i * PART, PART), :, pl.ds(pl.multiple_of(quarter(r) * lanes, lanes), lanes)],
            v.at[r, i],
            load_sem.at[i * 4 + r],
        )

    def to_core(i, p):
        return pltpu.make_async_remote_copy(
            src_ref=s1.at[i, p], dst_ref=r1.at[i, p],
            send_sem=d_send.at[i * 2 + p], recv_sem=d_recv.at[i * 2 + p],
            device_id=(core_peer, me), device_id_type=MESH,
        )

    def to_chip(i):
        return pltpu.make_async_remote_copy(
            src_ref=r1.at[i, 1], dst_ref=r2.at[i],
            send_sem=z_send.at[i], recv_sem=z_recv.at[i],
            device_id=(chip_peer, me), device_id_type=MESH,
        )

    def to_band(k, slot):
        return pltpu.make_async_remote_copy(
            src_ref=m.at[pl.ds(pl.multiple_of(k * 16, 16), 16)],
            dst_ref=r3.at[pl.ds(pl.multiple_of(slot * 16, 16), 16)],
            send_sem=a_send.at[k], recv_sem=a_recv.at[slot],
            device_id=(feed, k), device_id_type=MESH,
        )

    @pl.loop(0, parts)
    def _(i):
        for r in (3, 1, 2, 0):
            load(i, r).start()

    own_fine = pltpu.make_async_copy(
        fine_hbm.at[:, pl.ds(pl.multiple_of(me * width, width), width)], fd, side_sem.at[0]
    )
    own_fine.start()
    all_coarse = pltpu.make_async_copy(coarse_hbm, cd, side_sem.at[1])
    all_coarse.start()

    barrier = pltpu.get_barrier_semaphore()
    pl.semaphore_signal(barrier, inc=1, device_id=(core_peer, me), device_id_type=MESH)
    pl.semaphore_signal(barrier, inc=1, device_id=(chip_peer, me), device_id_type=MESH)

    @pl.loop(1, bands)
    def _(away):
        pl.semaphore_signal(
            barrier, inc=1, device_id=(feed, lax.rem(me + away, bands)), device_id_type=MESH
        )

    def widen(i):
        for r, p in ((3, 1), (1, 0)):
            load(i, r).wait()
            s1[i, p] = v[r, i].astype(jnp.float32).reshape(2, rows, lanes)

    def send_core(i):
        to_core(i, 1).start()
        to_core(i, 0).start()

    def pass_on(i):
        load(i, 2).wait()
        to_core(i, 1).wait_recv()
        r1[i, 1] = r1[i, 1] + v[2, i].astype(jnp.float32).reshape(2, rows, lanes)
        to_chip(i).start()

    widen(0)
    pl.semaphore_wait(barrier, bands + 1)
    send_core(0)

    @pl.loop(1, parts)
    def _(i):
        widen(i)
        send_core(i)
        pass_on(i - 1)

    pass_on(parts - 1)

    own_fine.wait()
    for delay in range(FINE_MAX + 1):
        chosen = jnp.where(fd[...] == delay, 1.0, 0.0).astype(jnp.bfloat16)
        mask[delay * groups : (delay + 1) * groups, :width] = chosen
        mask[delay * groups : (delay + 1) * groups, width:] = chosen

    all_coarse.wait()
    for q in range(rowsets):
        cdt[pl.ds(q, bands, stride=rowsets), :] = cd[q * LANES : (q + 1) * LANES, :].T
    lane = lax.broadcasted_iota(jnp.int32, (rowsets, LANES), 1)
    base = lane - lax.rem(lane, span) + lax.rem(lane, 16)
    first = lane - lax.rem(lane, 16)

    @pl.loop(0, bands)
    def _(s):
        codes = cdt[pl.ds(pl.multiple_of(s * rowsets, rowsets), rowsets), :]
        for j in range(16):
            idx[s * 16 + j] = base + gather_lanes(codes, first + j)

    def normalise(i, place):
        to_core(i, 0).wait_recv()
        load(i, 0).wait()
        to_chip(i).wait_recv()
        power = None
        for c in range(2):
            total = r1[i, 0, c] + v[0, i, c].astype(jnp.float32).reshape(rows, lanes) + r2[i, c]
            power = total * total if power is None else power + total * total
        power = power.reshape(PART, samples, lanes)
        level = jnp.sum(power, axis=1, keepdims=True) * (1.0 / samples)
        value = power * (1.0 / (level + epsilon)) - 1.0
        xt[place * rows : (place + 1) * rows, :] = value.reshape(rows, lanes)

    @pl.loop(0, parts * PART // BLOCK)
    def _(g):
        for place in range(BLOCK // PART):
            normalise(g * (BLOCK // PART) + place, place)
        for t in range(samples):
            value = xt[pl.ds(t, BLOCK, stride=samples), :]
            high = value.astype(jnp.bfloat16)
            low_part = (value - high.astype(jnp.float32)).astype(jnp.bfloat16)
            xhl[t, pl.ds(pl.multiple_of(g * BLOCK, BLOCK), BLOCK), :] = high
            xhl[t, pl.ds(pl.multiple_of(width + g * BLOCK, BLOCK), BLOCK), :] = low_part

    @pl.loop(0, parts)
    def _(i):
        to_core(i, 0).wait_send()
        to_core(i, 1).wait_send()

    terms = (FINE_MAX + 1) * groups

    @pl.loop(0, samples // 4)
    def _(i):
        for p in range(2):
            both = jnp.concatenate([xhl[i * 4 + p * 2], xhl[i * 4 + p * 2 + 1]], axis=1)
            product = jnp.dot(mask[...], both, preferred_element_type=jnp.float32)
            s1[i, p, 0, :terms, :] = product[:, :lanes]
            s1[i, p, 1, :terms, :] = product[:, lanes:]

    for t in range(span):
        total = None
        for delay in range(FINE_MAX + 1):
            at = t + delay
            term = s1[at // 4, at // 2 % 2, at % 2, delay * groups : (delay + 1) * groups, :]
            total = term if total is None else total + term
        o[pl.ds(t, groups, stride=span), :] = total

    for q in range(rowsets):
        m[pl.ds(q, lanes, stride=rowsets), :] = o[q * LANES : (q + 1) * LANES, :].T

    @pl.loop(1, bands)
    def _(away):
        to_band(lax.rem(me + away, bands), me).start()

    mine = pl.ds(pl.multiple_of(me * 16, 16), 16)
    r3[mine, :] = m[mine, :]

    def collect(s, totals):
        totals = list(totals)
        pair = [
            r3[pl.ds(pl.multiple_of(s * 16 + b * rowsets, rowsets), rowsets), :] for b in range(2)
        ]
        for j in range(16):
            index = idx[s * 16 + j]
            for b in range(2):
                totals[b * 16 + j] = totals[b * 16 + j] + gather_lanes(pair[b], index)
        return tuple(totals)

    def step(away, totals):
        s = lax.rem(me + bands - away, bands)
        to_band(s, s).wait_recv()
        return collect(s, totals)

    totals = collect(me, (jnp.zeros((rowsets, LANES), jnp.float32),) * 32)
    totals = lax.fori_loop(1, bands, step, totals)

    sample = lax.rem(lane, 16)

    def ahead(x, n):
        return pltpu.roll(x, LANES - n, 1)

    for b in range(2):
        best = [jnp.zeros((rowsets, LANES), jnp.float32)] * NWID
        for j in range(16):
            box = totals[b * 16 + j]
            for k in range(NWID):
                high = jnp.where(sample <= 16 - 2**k, box, -jnp.inf)
                for n in (8, 4, 2, 1):
                    high = jnp.maximum(high, ahead(high, n))
                if j:
                    high = pltpu.roll(high, j, 1)
                best[k] = jnp.where(sample == j, high, best[k])
                if k + 1 < NWID:
                    box = box + ahead(box, 2**k)
        for k in range(NWID):
            result = best[k] * (1.0 / math.sqrt(2**k * total_channels))
            for q in range(rowsets):
                out_ref[k, b : b + 1, q * LANES : (q + 1) * LANES] = result[q : q + 1, :]

    @pl.loop(1, bands)
    def _(away):
        k = lax.rem(me + away, bands)
        to_band(k, k).wait_send()

    @pl.loop(0, parts)
    def _(i):
        to_chip(i).wait_send()


def local(voltages, fine_delays, coarse_delays):
    _, _, channels, samples, beams = voltages.shape
    groups, total_channels = fine_delays.shape
    trials, bands = coarse_delays.shape
    lanes = beams // lax.axis_size("feed")
    parts = channels // PART
    rows = PART * samples
    f32, bf16, i32 = jnp.float32, jnp.bfloat16, jnp.int32
    dma = pltpu.SemaphoreType.DMA
    vmem = pltpu.VMEM
    return pl.pallas_call(
        functools.partial(kernel, bands, total_channels),
        out_shape=jax.ShapeDtypeStruct((NWID, beams // (lax.axis_size("feed") * bands), trials), f32),
        in_specs=[pl.BlockSpec(memory_space=pl.ANY)] * 3,
        out_specs=pl.BlockSpec(memory_space=pltpu.VMEM),
        scratch_shapes=[
            vmem((4, parts, 2, PART, samples, lanes), bf16),
            vmem((parts, 2, 2, rows, lanes), f32),
            vmem((parts, 2, 2, rows, lanes), f32),
            vmem((parts, 2, rows, lanes), f32),
            vmem((BLOCK * samples, lanes), f32),
            vmem((samples, 2 * channels, lanes), bf16),
            vmem(((FINE_MAX + 1) * groups, 2 * channels), bf16),
            vmem((groups, channels), i32),
            vmem((trials, bands), i32),
            vmem((bands * trials // LANES, LANES), i32),
            vmem((bands * 16, trials // LANES, LANES), i32),
            vmem((groups * (samples - FINE_MAX), lanes), f32),
            vmem((lanes * trials // LANES, LANES), f32),
            vmem((bands * 16, LANES), f32),
            dma((parts * 4,)),
            dma((2,)),
            dma((parts * 2,)),
            dma((parts * 2,)),
            dma((parts,)),
            dma((parts,)),
            dma((bands,)),
            dma((bands,)),
        ],
        compiler_params=pltpu.CompilerParams(
            collective_id=0, has_side_effects=True, vmem_limit_bytes=60 * 1024 * 1024
        ),
        cost_estimate=pl.CostEstimate(flops=10**9, bytes_accessed=11 * 10**6, transcendentals=0),
    )(voltages, fine_delays, coarse_delays)


def solution(mesh):
    in_specs = (P("feed", None, "chan", None, None), P(), P())
    out_specs = P(None, ("feed", "chan"), None)
    return jax.shard_map(local, mesh=mesh, in_specs=in_specs, out_specs=out_specs, check_vma=False)
```

time: 406 us -> 163 us (0.40); the launches traced: 401 us -> 162 us
  waiting for transfers between devices: 237 us -> 0 us
  Pallas kernels: 0 us -> 159 us
  local copies, waits for them, and re-layouts: 73.4 us -> 3.32 us
  matrix products: 37.5 us -> 0 us
  other arithmetic: 23.8 us -> 0 us
  between operations: 14.5 us -> 0.01 us
  starting transfers between devices: 13.9 us -> 0 us
    reduce_scatter x1 -> x0, waiting for transfers between devices: 184 us -> none  [local(): lax.psum_scatter(voltages[0].astype(jnp.float32), 'feed', scatter_dimensi...]
    pallas_call x0 -> x1, Pallas kernels: none -> 159 us  [local(): pl.pallas_call(functools.partial(kernel, bands, total_channels), out_shap...]
    all_to_all x1 -> x0, waiting for transfers between devices: 53.4 us -> none  [local(): lax.all_to_all(intensity, 'chan', split_axis=1, concat_axis=2, tiled=True)]
    slice x18 -> x0, local copies, waits for them, and re-layouts: 46.4 us -> none  [local(): partial_value[:, :, delay:delay + length]]
    dot_general x26 -> x0, matrix products: 37.5 us -> none  [the longest x9 25.6 us: local(): jnp.einsum('tbsc,gsc->sbtg', cube[delay:delay + span], chosen, precision=...]
    unnamed x87 -> x2, local copies, waits for them, and re-layouts: 26.4 us -> 3.32 us
    all_to_all x1 -> x0, starting transfers between devices: 13.9 us -> none  [local(): lax.all_to_all(intensity, 'chan', split_axis=1, concat_axis=2, tiled=True)]
    convert_element_type x1 -> x0, other arithmetic: 12.6 us -> none  [local(): voltages[0].astype(jnp.float32)]
  transfers between devices with their start and end apart: 2 -> 0, of which waited for: 2 -> 0; matrix products, arithmetic and copies ran while one was open for 3% -> 0% of each run, Pallas kernels for 0% -> 0%
where the time goes in v1:
time: 163 us; the launch traced here: 162 us
  Pallas kernels  159 us (98%)
  local copies, waits for them, and re-layouts  3.32 us (2%)
    pallas_call x1, Pallas kernels, local(): pl.pallas_call(functools.partial(kernel, bands, total_channels), out_shap...  159 us
    unnamed x2, local copies, waits for them, and re-layouts  3.32 us

profile of v1, /device:TPU:32, one launch (start us, length us, event | category | flops | bytes accessed | tf_op | source)
XLA Modules:
  0.0 162.2 jit_solution(17507456217314635977)
XLA Ops:
  0.0 1.9 %copy.4.coarse_hbm = s32[1024,64]{1,0:T(8,128)} copy(s32[1024,64]{0,1:T(8,128)} %param.5) | data formatting | bytes 524288 | tf_op args[2]
  1.9 158.9 %shard_map.37 = f32[4,2,1024]{2,1,0:T(2,128)} custom-call(bf16[1,2,128,40,512]{4,3,2,1,0:T(8,128)(2,1)} %v_hbm.1, s32[32,8192]{1,0:T(8,128)} %fine_hbm.1, s32[1024,64]{1,0:T(8,128)} %copy.4.coarse_hbm), custom_call_target="tpu_custom_call" | custom-call | flops 1000000000 | bytes 11000000 | tf_op jit(solution)/shard_map/pallas_call | solution.py:275
  160.9 1.4 copy.6

commit v2 on v1

--- a/solution.py
+++ b/solution.py
@@ -17,6 +17,7 @@
 PART = 8
 BLOCK = 16
 LANES = 128
+AHEAD = 4
 
 
 def gather_lanes(x, index):
@@ -36,7 +37,7 @@
     bands, total_channels,
     v_hbm, fine_hbm, coarse_hbm, out_ref,
     v, s1, r1, r2, xt, xhl, mask, fd, cd, cdt, idx, o, m, r3,
-    load_sem, side_sem, d_send, d_recv, z_send, z_recv, a_send, a_recv,
+    load_sem, side_sem, d_send, d_recv, z_send, z_recv, a_send, a_recv, met_sem,
 ):
     parts = v.shape[1]
     samples = v.shape[4]
@@ -45,8 +46,7 @@
     groups = fd.shape[0]
     width = fd.shape[1]
     span = samples - FINE_MAX
-    per_group = cd.shape[0] // groups
-    rowsets = cd.shape[0] // LANES
+    rowsets = cd.shape[1] // LANES
     feed = lax.axis_index("feed")
     me = lax.axis_index("chan")
     core, low = lax.rem(feed, 2), lax.div(feed, 2)
@@ -85,11 +85,30 @@
             device_id=(feed, k), device_id_type=MESH,
         )
 
-    @pl.loop(0, parts)
-    def _(i):
+    def fetch(i):
         for r in (3, 1, 2, 0):
             load(i, r).start()
 
+    fetch(0)
+
+    barrier = pltpu.get_barrier_semaphore()
+    pl.semaphore_signal(barrier, inc=1, device_id=(core_peer, me), device_id_type=MESH)
+    pl.semaphore_signal(barrier, inc=1, device_id=(chip_peer, me), device_id_type=MESH)
+
+    ring = min(bands, 4)
+    digit = lax.rem(me, ring)
+    friends = [[me - digit + lax.rem(digit + 1, ring)]]
+    if ring > 2:
+        friends[0].append(me - digit + lax.rem(digit + ring - 1, ring))
+    bit = ring
+    while bit < bands:
+        friends.append([me + (1 - 2 * lax.rem(lax.div(me, bit), 2)) * bit])
+        bit *= 2
+    for turn in friends:
+        for k in turn:
+            pl.semaphore_signal(barrier, inc=1, device_id=(feed, k), device_id_type=MESH)
+    for i in range(1, AHEAD):
+        fetch(i)
     own_fine = pltpu.make_async_copy(
         fine_hbm.at[:, pl.ds(pl.multiple_of(me * width, width), width)], fd, side_sem.at[0]
     )
@@ -97,24 +116,9 @@
     all_coarse = pltpu.make_async_copy(coarse_hbm, cd, side_sem.at[1])
     all_coarse.start()
 
-    barrier = pltpu.get_barrier_semaphore()
-    pl.semaphore_signal(barrier, inc=1, device_id=(core_peer, me), device_id_type=MESH)
-    pl.semaphore_signal(barrier, inc=1, device_id=(chip_peer, me), device_id_type=MESH)
-
-    @pl.loop(1, bands)
-    def _(away):
-        pl.semaphore_signal(
-            barrier, inc=1, device_id=(feed, lax.rem(me + away, bands)), device_id_type=MESH
-        )
-
-    def widen(i):
-        for r, p in ((3, 1), (1, 0)):
-            load(i, r).wait()
-            s1[i, p] = v[r, i].astype(jnp.float32).reshape(2, rows, lanes)
-
-    def send_core(i):
-        to_core(i, 1).start()
-        to_core(i, 0).start()
+    def widen(i, r, p):
+        load(i, r).wait()
+        s1[i, p] = v[r, i].astype(jnp.float32).reshape(2, rows, lanes)
 
     def pass_on(i):
         load(i, 2).wait()
@@ -122,17 +126,32 @@
         r1[i, 1] = r1[i, 1] + v[2, i].astype(jnp.float32).reshape(2, rows, lanes)
         to_chip(i).start()
 
-    widen(0)
-    pl.semaphore_wait(barrier, bands + 1)
-    send_core(0)
+    widen(0, 3, 1)
+    widen(0, 1, 0)
+    pl.semaphore_wait(barrier, 2 + sum(len(turn) for turn in friends))
+    to_core(0, 1).start()
+    to_core(0, 0).start()
 
     @pl.loop(1, parts)
     def _(i):
-        widen(i)
-        send_core(i)
+        @pl.when(i + AHEAD - 1 < parts)
+        def _():
+            fetch(i + AHEAD - 1)
+
+        for r, p in ((3, 1), (1, 0)):
+            widen(i, r, p)
+            to_core(i, p).start()
         pass_on(i - 1)
 
     pass_on(parts - 1)
+
+    for turn, ks in enumerate(friends):
+        if turn or ring > 2:
+            for k in ks:
+                pl.semaphore_signal(
+                    met_sem.at[turn], inc=1, device_id=(feed, k), device_id_type=MESH
+                )
+            pl.semaphore_wait(met_sem.at[turn], len(ks))
 
     own_fine.wait()
     for delay in range(FINE_MAX + 1):
@@ -142,7 +161,7 @@
 
     all_coarse.wait()
     for q in range(rowsets):
-        cdt[pl.ds(q, bands, stride=rowsets), :] = cd[q * LANES : (q + 1) * LANES, :].T
+        cdt[pl.ds(q, bands, stride=rowsets), :] = cd[:, q * LANES : (q + 1) * LANES]
     lane = lax.broadcasted_iota(jnp.int32, (rowsets, LANES), 1)
     base = lane - lax.rem(lane, span) + lax.rem(lane, 16)
     first = lane - lax.rem(lane, 16)
@@ -229,28 +248,30 @@
     totals = collect(me, (jnp.zeros((rowsets, LANES), jnp.float32),) * 32)
     totals = lax.fori_loop(1, bands, step, totals)
 
-    sample = lax.rem(lane, 16)
+    box = jnp.concatenate([totals[b * 16 + j] for j in range(16) for b in range(2)], axis=0)
+
+    def sample_of(x):
+        return lax.rem(lax.broadcasted_iota(jnp.int32, x.shape, 1), 16)
 
     def ahead(x, n):
         return pltpu.roll(x, LANES - n, 1)
 
-    for b in range(2):
-        best = [jnp.zeros((rowsets, LANES), jnp.float32)] * NWID
-        for j in range(16):
-            box = totals[b * 16 + j]
-            for k in range(NWID):
-                high = jnp.where(sample <= 16 - 2**k, box, -jnp.inf)
-                for n in (8, 4, 2, 1):
-                    high = jnp.maximum(high, ahead(high, n))
-                if j:
-                    high = pltpu.roll(high, j, 1)
-                best[k] = jnp.where(sample == j, high, best[k])
-                if k + 1 < NWID:
-                    box = box + ahead(box, 2**k)
-        for k in range(NWID):
-            result = best[k] * (1.0 / math.sqrt(2**k * total_channels))
+    for k in range(NWID):
+        best = jnp.where(sample_of(box) <= 16 - 2**k, box, -jnp.inf)
+        for n in (8, 4, 2, 1):
+            half = best.shape[0] // 2
+            a, b = best[:half], best[half:]
+            upper = lax.rem(lax.div(sample_of(a), n), 2) == 1
+            best = jnp.maximum(
+                jnp.where(upper, pltpu.roll(b, n, 1), a), jnp.where(upper, b, ahead(a, n))
+            )
+        result = best * (1.0 / math.sqrt(2**k * total_channels))
+        for b in range(2):
             for q in range(rowsets):
-                out_ref[k, b : b + 1, q * LANES : (q + 1) * LANES] = result[q : q + 1, :]
+                row = b * rowsets + q
+                out_ref[k, b : b + 1, q * LANES : (q + 1) * LANES] = result[row : row + 1, :]
+        if k + 1 < NWID:
+            box = box + ahead(box, 2**k)
 
     @pl.loop(1, bands)
     def _(away):
@@ -286,7 +307,7 @@
             vmem((samples, 2 * channels, lanes), bf16),
             vmem(((FINE_MAX + 1) * groups, 2 * channels), bf16),
             vmem((groups, channels), i32),
-            vmem((trials, bands), i32),
+            vmem((bands, trials), i32),
             vmem((bands * trials // LANES, LANES), i32),
             vmem((bands * 16, trials // LANES, LANES), i32),
             vmem((groups * (samples - FINE_MAX), lanes), f32),
@@ -300,12 +321,13 @@
             dma((parts,)),
             dma((bands,)),
             dma((bands,)),
+            pltpu.SemaphoreType.REGULAR((8,)),
         ],
         compiler_params=pltpu.CompilerParams(
             collective_id=0, has_side_effects=True, vmem_limit_bytes=60 * 1024 * 1024
         ),
         cost_estimate=pl.CostEstimate(flops=10**9, bytes_accessed=11 * 10**6, transcendentals=0),
-    )(voltages, fine_delays, coarse_delays)
+    )(voltages, fine_delays, coarse_delays.T)
 
 
 def solution(mesh):

time: 163 us -> 151 us (0.926)
  Pallas kernels: 159 us -> 149 us
  local copies, waits for them, and re-layouts: 3.32 us -> 1.38 us
    pallas_call x1, Pallas kernels: 159 us -> 149 us  [local(): pl.pallas_call(functools.partial(kernel, bands, total_channels), out_shap...]
    unnamed x2 -> x1, local copies, waits for them, and re-layouts: 3.32 us -> 1.38 us
where the time goes in v2:
time: 151 us
  Pallas kernels  149 us (99%)
    pallas_call x1, Pallas kernels, local(): pl.pallas_call(functools.partial(kernel, bands, total_channels), out_shap...  149 us

profile of v2, /device:TPU:32, one launch (start us, length us, event | category | flops | bytes accessed | tf_op | source)
XLA Modules:
  0.0 150.9 jit_solution(4968943349177361902)
XLA Ops:
  0.0 149.5 %shard_map.37 = f32[4,2,1024]{2,1,0:T(2,128)} custom-call(bf16[1,2,128,40,512]{4,3,2,1,0:T(8,128)(2,1)} %v_hbm.1, s32[32,8192]{1,0:T(8,128)} %fine_hbm.1, s32[64,1024]{1,0:T(8,128)} %bitcast.1), custom_call_target="tpu_custom_call" | custom-call | flops 1000000000 | bytes 11000000 | tf_op jit(solution)/shard_map/pallas_call | solution.py:296
  149.5 1.4 copy.5

commit v3 on v2

--- a/solution.py
+++ b/solution.py
@@ -203,8 +203,7 @@
 
     terms = (FINE_MAX + 1) * groups
 
-    @pl.loop(0, samples // 4)
-    def _(i):
+    for i in range(samples // 4):
         for p in range(2):
             both = jnp.concatenate([xhl[i * 4 + p * 2], xhl[i * 4 + p * 2 + 1]], axis=1)
             product = jnp.dot(mask[...], both, preferred_element_type=jnp.float32)
@@ -240,13 +239,18 @@
                 totals[b * 16 + j] = totals[b * 16 + j] + gather_lanes(pair[b], index)
         return tuple(totals)
 
-    def step(away, totals):
-        s = lax.rem(me + bands - away, bands)
-        to_band(s, s).wait_recv()
-        return collect(s, totals)
+    together = max(n for n in range(1, 8) if (bands - 1) % n == 0)
+
+    def step(turn, totals):
+        sources = [lax.rem(me + bands - 1 - turn * together - n, bands) for n in range(together)]
+        for s in sources:
+            to_band(s, s).wait_recv()
+        for s in sources:
+            totals = collect(s, totals)
+        return totals
 
     totals = collect(me, (jnp.zeros((rowsets, LANES), jnp.float32),) * 32)
-    totals = lax.fori_loop(1, bands, step, totals)
+    totals = lax.fori_loop(0, (bands - 1) // together, step, totals)
 
     box = jnp.concatenate([totals[b * 16 + j] for j in range(16) for b in range(2)], axis=0)
 

time: 151 us -> 149 us (0.987)
  Pallas kernels: 149 us -> 146 us
    pallas_call x1, Pallas kernels: 149 us -> 146 us  [local(): pl.pallas_call(functools.partial(kernel, bands, total_channels), out_shap...]
where the time goes in v3:
time: 149 us; the launch traced here: 148 us
  Pallas kernels  146 us (98%)
    pallas_call x1, Pallas kernels, local(): pl.pallas_call(functools.partial(kernel, bands, total_channels), out_shap...  146 us

profile of v3, /device:TPU:32, one launch (start us, length us, event | category | flops | bytes accessed | tf_op | source)
XLA Modules:
  0.0 147.7 jit_solution(16830333239774681227)
XLA Ops:
  0.0 146.3 %shard_map.37 = f32[4,2,1024]{2,1,0:T(2,128)} custom-call(bf16[1,2,128,40,512]{4,3,2,1,0:T(8,128)(2,1)} %v_hbm.1, s32[32,8192]{1,0:T(8,128)} %fine_hbm.1, s32[64,1024]{1,0:T(8,128)} %bitcast.1), custom_call_target="tpu_custom_call" | custom-call | flops 1000000000 | bytes 11000000 | tf_op jit(solution)/shard_map/pallas_call | solution.py:300
  146.3 1.4 copy.5

commit v4 on v3

--- a/solution.py
+++ b/solution.py
@@ -36,13 +36,14 @@
 def kernel(
     bands, total_channels,
     v_hbm, fine_hbm, coarse_hbm, out_ref,
-    v, s1, r1, r2, xt, xhl, mask, fd, cd, cdt, idx, o, m, r3,
+    v, s1, r1, zs, r2, xt, xhl, mask, fd, cd, cdt, idx, o, m, r3,
     load_sem, side_sem, d_send, d_recv, z_send, z_recv, a_send, a_recv, met_sem,
 ):
     parts = v.shape[1]
     samples = v.shape[4]
     lanes = v.shape[5]
     rows = PART * samples
+    packed = rows // 2
     groups = fd.shape[0]
     width = fd.shape[1]
     span = samples - FINE_MAX
@@ -70,19 +71,40 @@
             device_id=(core_peer, me), device_id_type=MESH,
         )
 
-    def to_chip(i):
+    def to_chip(h, i):
         return pltpu.make_async_remote_copy(
-            src_ref=r1.at[i, 1], dst_ref=r2.at[i],
-            send_sem=z_send.at[i], recv_sem=z_recv.at[i],
+            src_ref=zs.at[h, i], dst_ref=r2.at[h, i],
+            send_sem=z_send.at[h * parts + i], recv_sem=z_recv.at[h * parts + i],
             device_id=(chip_peer, me), device_id_type=MESH,
         )
 
-    def to_band(k, slot):
+    spot, plane = lax.rem(me, 4), lax.div(me, 4)
+    planes = bands // 4
+    way = 2 * low - 1
+
+    def wrap(x):
+        return lax.rem(x + 16, 4)
+
+    def goal(h, n):
+        which = lax.rem(n, 2)
+        k = lax.rem(plane + lax.div(n, 2), planes) * 4 + wrap(spot + (h + which) * way)
+        return k, lax.rem(low + which, 2) * 2 + core
+
+    def origin(h, n):
+        which = lax.rem(n, 2)
+        return lax.rem(plane + planes - lax.div(n, 2), planes) * 4 + wrap(
+            spot - (h + which) * way * (1 - 2 * which)
+        )
+
+    def block(k):
+        return pl.ds(pl.multiple_of(k * 16, 16), 16)
+
+    def to_band(h, n, slot):
+        k, owner = goal(h, n)
         return pltpu.make_async_remote_copy(
-            src_ref=m.at[pl.ds(pl.multiple_of(k * 16, 16), 16)],
-            dst_ref=r3.at[pl.ds(pl.multiple_of(slot * 16, 16), 16)],
-            send_sem=a_send.at[k], recv_sem=a_recv.at[slot],
-            device_id=(feed, k), device_id_type=MESH,
+            src_ref=m.at[h, block(k)], dst_ref=r3.at[block(slot)],
+            send_sem=a_send.at[h * (bands // 2) + n], recv_sem=a_recv.at[slot],
+            device_id=(owner, k), device_id_type=MESH,
         )
 
     def fetch(i):
@@ -120,11 +142,32 @@
         load(i, r).wait()
         s1[i, p] = v[r, i].astype(jnp.float32).reshape(2, rows, lanes)
 
+    where = lax.broadcasted_iota(jnp.int32, (packed, lanes), 1)
+    slot = lax.div(lax.rem(where, 8), 2)
+
+    def turned(x):
+        at = lax.rem(lax.broadcasted_iota(jnp.int32, x.shape, 1), 8)
+        return jnp.where(at < 4, pltpu.roll(x, lanes - 4, 1), pltpu.roll(x, 4, 1))
+
+    def pack(near, far, h, step):
+        here = slot == wrap(spot + h * step)
+        also = slot == wrap(spot + (h + 1) * step)
+        first = jnp.where(here, near[:packed], far[:packed])
+        second = jnp.where(here, near[packed:], far[packed:])
+        return jnp.where(jnp.logical_or(here, also), first, turned(second))
+
     def pass_on(i):
-        load(i, 2).wait()
-        to_core(i, 1).wait_recv()
-        r1[i, 1] = r1[i, 1] + v[2, i].astype(jnp.float32).reshape(2, rows, lanes)
-        to_chip(i).start()
+        for r in (2, 0):
+            load(i, r).wait()
+        for p in (1, 0):
+            to_core(i, p).wait_recv()
+        for c in range(2):
+            own = r1[i, 0, c] + v[0, i, c].astype(jnp.float32).reshape(rows, lanes)
+            other = r1[i, 1, c] + v[2, i, c].astype(jnp.float32).reshape(rows, lanes)
+            for h in range(2):
+                zs[h, i, c] = pack(other, own, h, -way)
+                r1[i, 0, c, h * packed : (h + 1) * packed, :] = pack(own, other, h, way)
+        to_chip(0, i).start()
 
     widen(0, 3, 1)
     widen(0, 1, 0)
@@ -153,9 +196,20 @@
                 )
             pl.semaphore_wait(met_sem.at[turn], len(ks))
 
+    pl.semaphore_signal(
+        met_sem.at[len(friends)], inc=1, device_id=(chip_peer, me), device_id_type=MESH
+    )
+    pl.semaphore_wait(met_sem.at[len(friends)], 1)
+
     own_fine.wait()
+    place_of = lax.broadcasted_iota(jnp.int32, (8, width), 1)
+    in_four = lax.rem(lax.div(place_of, 4), 4)
+    order = place_of + jnp.where(in_four == 1, 4, 0) - jnp.where(in_four == 2, 4, 0)
+    delays = jnp.concatenate(
+        [gather_lanes(fd[q : q + 8, :], order) for q in range(0, groups, 8)], axis=0
+    )
     for delay in range(FINE_MAX + 1):
-        chosen = jnp.where(fd[...] == delay, 1.0, 0.0).astype(jnp.bfloat16)
+        chosen = jnp.where(delays == delay, 1.0, 0.0).astype(jnp.bfloat16)
         mask[delay * groups : (delay + 1) * groups, :width] = chosen
         mask[delay * groups : (delay + 1) * groups, width:] = chosen
 
@@ -172,30 +226,46 @@
         for j in range(16):
             idx[s * 16 + j] = base + gather_lanes(codes, first + j)
 
-    def normalise(i, place):
-        to_core(i, 0).wait_recv()
-        load(i, 0).wait()
-        to_chip(i).wait_recv()
+    def normalise(h, i, place):
+        to_chip(h, i).wait_recv()
         power = None
         for c in range(2):
-            total = r1[i, 0, c] + v[0, i, c].astype(jnp.float32).reshape(rows, lanes) + r2[i, c]
+            half = pl.ds(pl.multiple_of(h * packed, 8), packed)
+            total = r1[i, 0, c, half, :] + r2[h, i, c]
             power = total * total if power is None else power + total * total
-        power = power.reshape(PART, samples, lanes)
+        power = power.reshape(PART // 2, samples, lanes)
         level = jnp.sum(power, axis=1, keepdims=True) * (1.0 / samples)
         value = power * (1.0 / (level + epsilon)) - 1.0
-        xt[place * rows : (place + 1) * rows, :] = value.reshape(rows, lanes)
-
-    @pl.loop(0, parts * PART // BLOCK)
-    def _(g):
-        for place in range(BLOCK // PART):
-            normalise(g * (BLOCK // PART) + place, place)
+        xt[place * packed : (place + 1) * packed, :] = value.reshape(packed, lanes)
+
+    each = BLOCK // PART
+    blocks = parts // each
+
+    def prepare(h, g):
+        for place in range(each):
+            normalise(h, g * each + place, place)
         for t in range(samples):
-            value = xt[pl.ds(t, BLOCK, stride=samples), :]
+            value = xt[pl.ds(t, BLOCK // 2, stride=samples), :]
+            value = jnp.concatenate([value, turned(value)], axis=0)
             high = value.astype(jnp.bfloat16)
             low_part = (value - high.astype(jnp.float32)).astype(jnp.bfloat16)
             xhl[t, pl.ds(pl.multiple_of(g * BLOCK, BLOCK), BLOCK), :] = high
             xhl[t, pl.ds(pl.multiple_of(width + g * BLOCK, BLOCK), BLOCK), :] = low_part
 
+    def release(g):
+        for place in range(each):
+            to_chip(1, g * each + place).start()
+
+    @pl.loop(0, blocks)
+    def _(g):
+        @pl.when(g == blocks - 2)
+        def _():
+            release(0)
+
+        prepare(0, g)
+
+    release(1)
+
     @pl.loop(0, parts)
     def _(i):
         to_core(i, 0).wait_send()
@@ -203,30 +273,36 @@
 
     terms = (FINE_MAX + 1) * groups
 
-    for i in range(samples // 4):
-        for p in range(2):
-            both = jnp.concatenate([xhl[i * 4 + p * 2], xhl[i * 4 + p * 2 + 1]], axis=1)
-            product = jnp.dot(mask[...], both, preferred_element_type=jnp.float32)
-            s1[i, p, 0, :terms, :] = product[:, :lanes]
-            s1[i, p, 1, :terms, :] = product[:, lanes:]
-
-    for t in range(span):
-        total = None
-        for delay in range(FINE_MAX + 1):
-            at = t + delay
-            term = s1[at // 4, at // 2 % 2, at % 2, delay * groups : (delay + 1) * groups, :]
-            total = term if total is None else total + term
-        o[pl.ds(t, groups, stride=span), :] = total
-
-    for q in range(rowsets):
-        m[pl.ds(q, lanes, stride=rowsets), :] = o[q * LANES : (q + 1) * LANES, :].T
-
-    @pl.loop(1, bands)
-    def _(away):
-        to_band(lax.rem(me + away, bands), me).start()
-
-    mine = pl.ds(pl.multiple_of(me * 16, 16), 16)
-    r3[mine, :] = m[mine, :]
+    def finish(h):
+        for i in range(samples // 4):
+            for p in range(2):
+                both = jnp.concatenate([xhl[i * 4 + p * 2], xhl[i * 4 + p * 2 + 1]], axis=1)
+                product = jnp.dot(mask[...], both, preferred_element_type=jnp.float32)
+                s1[i, p, 0, :terms, :] = product[:, :lanes]
+                s1[i, p, 1, :terms, :] = product[:, lanes:]
+
+        for t in range(span):
+            total = None
+            for delay in range(FINE_MAX + 1):
+                at = t + delay
+                term = s1[at // 4, at // 2 % 2, at % 2, delay * groups : (delay + 1) * groups, :]
+                total = term if total is None else total + term
+            o[pl.ds(t, groups, stride=span), :] = total
+
+        for q in range(rowsets):
+            m[h, pl.ds(q, lanes, stride=rowsets), :] = o[q * LANES : (q + 1) * LANES, :].T
+
+        @pl.loop(1 - h, bands // 2)
+        def _(n):
+            to_band(h, n, me).start()
+
+    finish(0)
+    r3[block(me), :] = m[0, block(me), :]
+
+    @pl.loop(0, blocks - 2)
+    def _(g):
+        release(g + 2)
+        prepare(1, g)
 
     def collect(s, totals):
         totals = list(totals)
@@ -239,18 +315,37 @@
                 totals[b * 16 + j] = totals[b * 16 + j] + gather_lanes(pair[b], index)
         return tuple(totals)
 
-    together = max(n for n in range(1, 8) if (bands - 1) % n == 0)
-
-    def step(turn, totals):
-        sources = [lax.rem(me + bands - 1 - turn * together - n, bands) for n in range(together)]
-        for s in sources:
-            to_band(s, s).wait_recv()
+    together = min(8, bands // 2)
+
+    def step(h, turn, totals):
+        sources = []
+        for n in range(together):
+            n += turn * together
+            s = origin(h, n)
+            sources.append(s)
+            if h == 0:
+
+                @pl.when(n > 0)
+                def _():
+                    to_band(h, n, s).wait()
+            else:
+                to_band(h, n, s).wait()
         for s in sources:
             totals = collect(s, totals)
         return totals
 
-    totals = collect(me, (jnp.zeros((rowsets, LANES), jnp.float32),) * 32)
-    totals = lax.fori_loop(0, (bands - 1) // together, step, totals)
+    totals = (jnp.zeros((rowsets, LANES), jnp.float32),) * 32
+    turns = bands // 2 // together
+    totals = lax.fori_loop(0, turns, functools.partial(step, 0), totals)
+    for g in range(blocks - 2, blocks):
+        prepare(1, g)
+    finish(1)
+
+    @pl.loop(0, 2 * parts)
+    def _(i):
+        to_chip(lax.div(i, parts), lax.rem(i, parts)).wait_send()
+
+    totals = lax.fori_loop(0, turns, functools.partial(step, 1), totals)
 
     box = jnp.concatenate([totals[b * 16 + j] for j in range(16) for b in range(2)], axis=0)
 
@@ -276,15 +371,6 @@
                 out_ref[k, b : b + 1, q * LANES : (q + 1) * LANES] = result[row : row + 1, :]
         if k + 1 < NWID:
             box = box + ahead(box, 2**k)
-
-    @pl.loop(1, bands)
-    def _(away):
-        k = lax.rem(me + away, bands)
-        to_band(k, k).wait_send()
-
-    @pl.loop(0, parts)
-    def _(i):
-        to_chip(i).wait_send()
 
 
 def local(voltages, fine_delays, coarse_delays):
@@ -306,8 +392,9 @@
             vmem((4, parts, 2, PART, samples, lanes), bf16),
             vmem((parts, 2, 2, rows, lanes), f32),
             vmem((parts, 2, 2, rows, lanes), f32),
-            vmem((parts, 2, rows, lanes), f32),
-            vmem((BLOCK * samples, lanes), f32),
+            vmem((2, parts, 2, rows // 2, lanes), f32),
+            vmem((2, parts, 2, rows // 2, lanes), f32),
+            vmem((BLOCK // 2 * samples, lanes), f32),
             vmem((samples, 2 * channels, lanes), bf16),
             vmem(((FINE_MAX + 1) * groups, 2 * channels), bf16),
             vmem((groups, channels), i32),
@@ -315,14 +402,14 @@
             vmem((bands * trials // LANES, LANES), i32),
             vmem((bands * 16, trials // LANES, LANES), i32),
             vmem((groups * (samples - FINE_MAX), lanes), f32),
-            vmem((lanes * trials // LANES, LANES), f32),
+            vmem((2, lanes * trials // LANES, LANES), f32),
             vmem((bands * 16, LANES), f32),
             dma((parts * 4,)),
             dma((2,)),
             dma((parts * 2,)),
             dma((parts * 2,)),
-            dma((parts,)),
-            dma((parts,)),
+            dma((2 * parts,)),
+            dma((2 * parts,)),
             dma((bands,)),
             dma((bands,)),
             pltpu.SemaphoreType.REGULAR((8,)),

time: 149 us -> 145 us (0.973)
  Pallas kernels: 146 us -> 143 us
    pallas_call x1, Pallas kernels: 146 us -> 143 us  [local(): pl.pallas_call(functools.partial(kernel, bands, total_channels), out_shap...]
where the time goes in v4:
time: 145 us; the launch traced here: 144 us
  Pallas kernels  143 us (99%)
    pallas_call x1, Pallas kernels, local(): pl.pallas_call(functools.partial(kernel, bands, total_channels), out_shap...  143 us

profile of v4, /device:TPU:32, one launch (start us, length us, event | category | flops | bytes accessed | tf_op | source)
XLA Modules:
  0.0 144.4 jit_solution(17754373873012742342)
XLA Ops:
  0.0 143.1 %shard_map.37 = f32[4,2,1024]{2,1,0:T(2,128)} custom-call(bf16[1,2,128,40,512]{4,3,2,1,0:T(8,128)(2,1)} %v_hbm.1, s32[32,8192]{1,0:T(8,128)} %fine_hbm.1, s32[64,1024]{1,0:T(8,128)} %bitcast.1), custom_call_target="tpu_custom_call" | custom-call | flops 1000000000 | bytes 11000000 | tf_op jit(solution)/shard_map/pallas_call | solution.py:386
  143.1 1.4 copy.5

commit v5 on v4

--- a/solution.py
+++ b/solution.py
@@ -149,6 +149,10 @@
         at = lax.rem(lax.broadcasted_iota(jnp.int32, x.shape, 1), 8)
         return jnp.where(at < 4, pltpu.roll(x, lanes - 4, 1), pltpu.roll(x, 4, 1))
 
+    def kept(h, count):
+        at = lax.div(lax.rem(lax.broadcasted_iota(jnp.int32, (count, lanes), 1), 8), 2)
+        return jnp.logical_or(at == wrap(spot + h * way), at == wrap(spot + (h + 1) * way))
+
     def pack(near, far, h, step):
         here = slot == wrap(spot + h * step)
         also = slot == wrap(spot + (h + 1) * step)
@@ -161,19 +165,28 @@
             load(i, r).wait()
         for p in (1, 0):
             to_core(i, p).wait_recv()
+        def sums(c):
+            return [
+                r1[i, p, c] + v[2 * p, i, c].astype(jnp.float32).reshape(rows, lanes)
+                for p in range(2)
+            ]
+
         for c in range(2):
-            own = r1[i, 0, c] + v[0, i, c].astype(jnp.float32).reshape(rows, lanes)
-            other = r1[i, 1, c] + v[2, i, c].astype(jnp.float32).reshape(rows, lanes)
+            own, other = sums(c)
+            zs[0, i, c] = pack(other, own, 0, -way)
+        to_chip(0, i).start()
+        for c in range(2):
+            own, other = sums(c)
+            zs[1, i, c] = pack(other, own, 1, -way)
             for h in range(2):
-                zs[h, i, c] = pack(other, own, h, -way)
                 r1[i, 0, c, h * packed : (h + 1) * packed, :] = pack(own, other, h, way)
-        to_chip(0, i).start()
 
     widen(0, 3, 1)
     widen(0, 1, 0)
     pl.semaphore_wait(barrier, 2 + sum(len(turn) for turn in friends))
     to_core(0, 1).start()
     to_core(0, 0).start()
+    pass_on(0)
 
     @pl.loop(1, parts)
     def _(i):
@@ -184,9 +197,7 @@
         for r, p in ((3, 1), (1, 0)):
             widen(i, r, p)
             to_core(i, p).start()
-        pass_on(i - 1)
-
-    pass_on(parts - 1)
+        pass_on(i)
 
     for turn, ks in enumerate(friends):
         if turn or ring > 2:
@@ -244,9 +255,13 @@
     def prepare(h, g):
         for place in range(each):
             normalise(h, g * each + place, place)
-        for t in range(samples):
-            value = xt[pl.ds(t, BLOCK // 2, stride=samples), :]
-            value = jnp.concatenate([value, turned(value)], axis=0)
+        keep = kept(h, BLOCK // 2)
+        for t in range(samples // 2):
+            even = xt[pl.ds(2 * t, BLOCK // 2, stride=samples), :]
+            odd = xt[pl.ds(2 * t + 1, BLOCK // 2, stride=samples), :]
+            value = jnp.concatenate(
+                [jnp.where(keep, even, turned(odd)), jnp.where(keep, turned(even), odd)], axis=0
+            )
             high = value.astype(jnp.bfloat16)
             low_part = (value - high.astype(jnp.float32)).astype(jnp.bfloat16)
             xhl[t, pl.ds(pl.multiple_of(g * BLOCK, BLOCK), BLOCK), :] = high
@@ -274,20 +289,31 @@
     terms = (FINE_MAX + 1) * groups
 
     def finish(h):
-        for i in range(samples // 4):
+        for i in range(samples // 8):
             for p in range(2):
                 both = jnp.concatenate([xhl[i * 4 + p * 2], xhl[i * 4 + p * 2 + 1]], axis=1)
                 product = jnp.dot(mask[...], both, preferred_element_type=jnp.float32)
                 s1[i, p, 0, :terms, :] = product[:, :lanes]
                 s1[i, p, 1, :terms, :] = product[:, lanes:]
 
-        for t in range(span):
-            total = None
-            for delay in range(FINE_MAX + 1):
-                at = t + delay
-                term = s1[at // 4, at // 2 % 2, at % 2, delay * groups : (delay + 1) * groups, :]
-                total = term if total is None else total + term
-            o[pl.ds(t, groups, stride=span), :] = total
+        keep = kept(h, groups)
+
+        def term(at, delay):
+            rows_of = slice(delay * groups, (delay + 1) * groups)
+            return s1[at // 4, at // 2 % 2, at % 2, rows_of, :]
+
+        for t in range(span // 2):
+            total = term(t, 0)
+            for delay in range(2, FINE_MAX + 1, 2):
+                total = total + term(t + delay // 2, delay)
+            crossed = None
+            for delay in range(1, FINE_MAX + 1, 2):
+                at = t + delay // 2
+                value = jnp.where(keep, term(at + 1, delay), term(at, delay))
+                crossed = value if crossed is None else crossed + value
+            total = total + turned(crossed)
+            o[pl.ds(2 * t, groups, stride=span), :] = total
+            o[pl.ds(2 * t + 1, groups, stride=span), :] = turned(total)
 
         for q in range(rowsets):
             m[h, pl.ds(q, lanes, stride=rowsets), :] = o[q * LANES : (q + 1) * LANES, :].T
@@ -366,9 +392,8 @@
             )
         result = best * (1.0 / math.sqrt(2**k * total_channels))
         for b in range(2):
-            for q in range(rowsets):
-                row = b * rowsets + q
-                out_ref[k, b : b + 1, q * LANES : (q + 1) * LANES] = result[row : row + 1, :]
+            part = result[b * rowsets : (b + 1) * rowsets]
+            out_ref[pl.ds(k * 2 * rowsets + b, rowsets, stride=2), :] = part
         if k + 1 < NWID:
             box = box + ahead(box, 2**k)
 
@@ -383,9 +408,9 @@
     f32, bf16, i32 = jnp.float32, jnp.bfloat16, jnp.int32
     dma = pltpu.SemaphoreType.DMA
     vmem = pltpu.VMEM
-    return pl.pallas_call(
+    largest = pl.pallas_call(
         functools.partial(kernel, bands, total_channels),
-        out_shape=jax.ShapeDtypeStruct((NWID, beams // (lax.axis_size("feed") * bands), trials), f32),
+        out_shape=jax.ShapeDtypeStruct((NWID * 2 * trials // LANES, LANES), f32),
         in_specs=[pl.BlockSpec(memory_space=pl.ANY)] * 3,
         out_specs=pl.BlockSpec(memory_space=pltpu.VMEM),
         scratch_shapes=[
@@ -395,7 +420,7 @@
             vmem((2, parts, 2, rows // 2, lanes), f32),
             vmem((2, parts, 2, rows // 2, lanes), f32),
             vmem((BLOCK // 2 * samples, lanes), f32),
-            vmem((samples, 2 * channels, lanes), bf16),
+            vmem((samples // 2, 2 * channels, lanes), bf16),
             vmem(((FINE_MAX + 1) * groups, 2 * channels), bf16),
             vmem((groups, channels), i32),
             vmem((bands, trials), i32),
@@ -419,6 +444,8 @@
         ),
         cost_estimate=pl.CostEstimate(flops=10**9, bytes_accessed=11 * 10**6, transcendentals=0),
     )(voltages, fine_delays, coarse_delays.T)
+    largest = largest.reshape(NWID, trials // LANES, 2, LANES)
+    return jnp.transpose(largest, (0, 2, 1, 3)).reshape(NWID, 2, trials)
 
 
 def solution(mesh):

time: 145 us -> 145 us (level)
  no operation moved by 1% of the time
where the time goes in v5:
time: 145 us; the launch traced here: 144 us
  Pallas kernels  143 us (99%)
    pallas_call x1, Pallas kernels, local(): pl.pallas_call(functools.partial(kernel, bands, total_channels), out_shap...  143 us

profile of v5, /device:TPU:32, one launch (start us, length us, event | category | flops | bytes accessed | tf_op | source)
XLA Modules:
  0.0 143.9 jit_solution(9858088022187017912)
XLA Ops:
  0.0 142.5 %shard_map.37 = f32[64,128]{1,0:T(8,128)} custom-call(bf16[1,2,128,40,512]{4,3,2,1,0:T(8,128)(2,1)} %v_hbm.1, s32[32,8192]{1,0:T(8,128)} %fine_hbm.1, s32[64,1024]{1,0:T(8,128)} %bitcast.6), custom_call_target="tpu_custom_call" | custom-call | flops 1000000000 | bytes 11000000 | tf_op jit(solution)/shard_map/pallas_call | solution.py:411
  142.6 1.4 copy.6
